TPU v7x, 32 devices: a whole 2x2x4 slice. The times are simulated.
32 devices in a mesh: groups: 2 (over x), seq: 16 (over z, y, core).
Axes of the slice: x: 2, y: 2, z: 4, core: 2. Of those that a mesh axis runs over, the one named last changes fastest.
Arguments:
- queries: bfloat16 [8192, 2048], P(('groups', 'seq')), parts along dimension 0, may hold values from -9 to 9
- keys: bfloat16 [8192, 512], P(('groups', 'seq')), parts along dimension 0, may hold values from -9 to 9
- values: bfloat16 [8192, 512], P(('groups', 'seq')), parts along dimension 0, may hold values from -6 to 6
- segment: int32 [8192], P(('groups', 'seq')), parts along dimension 0, may hold values from 0 to 10, never falling along the last dimension, each value on 1 to 769 neighbouring positions
- out_weight: bfloat16 [2048, 4096], P('seq'), may hold values from -0.125 to 0.125
Outputs:
- projected: bfloat16 [8192, 4096], P(('groups', 'seq')), parts along dimension 0
There are 2 independent parts, one for each index of `groups`. A program takes and returns all parts, laid end to end along the dimension named above; an argument that names none is the same for every part. Nothing has to cross between parts.
Inputs may be any that keep to these rules, and one draw needn't show every extreme that they name: `segment`: document numbers never fall along the stretch; every document has 1 to 769 tokens.
All inputs are finite; a program needn't handle non-finite values.
Results may differ from a plain program's by a relative error of at most 0.0053.
Values may be sent and summed in bfloat16 or wider, within the bound.
A program may use at most 128 MiB of HBM per device.

v0:
```python
import jax
import jax.numpy as jnp
from jax import lax
from jax.sharding import PartitionSpec as P

HEADS = 16
KV_HEADS = 4
HEAD = 128
SPAN = 4


def shifted(block, axis, distance):
    devices = range(lax.axis_size(axis))
    route = [(i - distance, i) for i in devices if i - distance in devices]
    return lax.ppermute(block, axis, route)


def one_head(query_group, key_head, value_head, live_mask):
    score_scale = HEAD ** (-0.5)
    scores = (
        jnp.einsum("thd,sd->ths", query_group, key_head, preferred_element_type=jnp.float32)
        * score_scale
    )
    scores = jnp.where(live_mask[:, None, :], scores, -jnp.inf)
    row_max = jnp.max(scores, axis=-1, keepdims=True)
    weights = jnp.exp(scores - row_max)
    weight_sum = jnp.sum(weights, axis=-1, keepdims=True)
    probabilities = weights.astype(jnp.bfloat16)
    head_mix = jnp.einsum(
        "ths,sd->thd", probabilities, value_head, preferred_element_type=jnp.float32
    )
    return head_mix / weight_sum


def attend(queries_block, keys_window, values_window, live_mask):
    row_count = queries_block.shape[0]
    window_rows = keys_window.shape[0]
    group_size = HEADS // KV_HEADS
    query_heads = queries_block.reshape(row_count, KV_HEADS, group_size, HEAD).transpose(1, 0, 2, 3)
    key_heads = keys_window.reshape(window_rows, KV_HEADS, HEAD).transpose(1, 0, 2)
    value_heads = values_window.reshape(window_rows, KV_HEADS, HEAD).transpose(1, 0, 2)

    def per_group(operands):
        return one_head(operands[0], operands[1], operands[2], live_mask)

    head_outputs = lax.map(per_group, (query_heads, key_heads, value_heads))
    return head_outputs.transpose(1, 0, 2, 3).reshape(row_count, HEADS * HEAD).astype(jnp.bfloat16)


def body(queries, keys, values, segment, out_weight):
    row_count = queries.shape[0]
    shard_index = lax.axis_index("seq")
    current = (keys, values, segment)
    collected = [current]
    for hop_count in range(SPAN - 1):
        current = shifted((current[0], current[1], current[2]), "seq", 1)
        collected.insert(0, current)
    window = tuple(
        (jnp.concatenate([arrival[member] for arrival in collected], axis=0) for member in range(3))
    )
    keys_window, values_window, segment_window = window
    query_pos = shard_index * row_count + jnp.arange(row_count, dtype=jnp.int32)
    key_pos = (shard_index - (SPAN - 1)) * row_count + jnp.arange(SPAN * row_count, dtype=jnp.int32)
    live_mask = (
        (segment[:, None] == segment_window[None, :])
        & (key_pos[None, :] <= query_pos[:, None])
        & (key_pos[None, :] >= 0)
    )
    attention = attend(queries, keys_window, values_window, live_mask)
    result = jnp.dot(
        attention,
        lax.all_gather(out_weight, "seq", axis=0, tiled=True),
        preferred_element_type=jnp.float32,
    )
    return result.astype(jnp.bfloat16)


def solution(mesh):
    in_specs = (
        P(("groups", "seq"), None),
        P(("groups", "seq"), None),
        P(("groups", "seq"), None),
        P(("groups", "seq")),
        P("seq", None),
    )
    out_specs = P(("groups", "seq"), None)
    return jax.shard_map(body, mesh=mesh, in_specs=in_specs, out_specs=out_specs, check_vma=False)
```

profile of v0, /device:TPU:0, one launch (start us, length us, event | category | flops | bytes accessed | tf_op | source)
XLA Modules:
  0.0 166.5 jit_solution(8321568713052091518)
XLA Ops:
  6.5 0.7 all-gather.2.cloned.1.call-update
  7.3 1.1 copy.7
  8.3 2.4 %collective-permute-start.3 = (bf16[256,512]{0,1:T(8,128)(2,1)S(1)}, bf16[256,512]{0,1:T(8,128)(2,1)S(1)}, u32[]{:S(2)}, u32[]{:S(2)}) collective-permute-start(bf16[256,512]{0,1:T(8,128)(2,1)S(1)} %copy.7), channel_id=1, source_target_pairs={{0,1},{1,2},{2,3},{3,4},{4,5},{5,6},{6,7},{7,8},{8,9},{9,10},{10,1... | collective-permute-start | bytes 786440 | tf_op jit(solution)/shard_map/ppermute | solution.py:15
  10.7 1.1 copy.9
  11.8 4.5 %collective-permute-start.6 = (bf16[256,512]{0,1:T(8,128)(2,1)S(1)}, bf16[256,512]{0,1:T(8,128)(2,1)S(1)}, u32[]{:S(2)}, u32[]{:S(2)}) collective-permute-start(bf16[256,512]{0,1:T(8,128)(2,1)S(1)} %copy.9), channel_id=1, source_target_pairs={{0,1},{1,2},{2,3},{3,4},{4,5},{5,6},{6,7},{7,8},{8,9},{9,10},{10,1... | collective-permute-start | bytes 786440 | tf_op jit(solution)/shard_map/ppermute | solution.py:15
  16.4 2.2 %collective-permute-start.4 = (bf16[256,512]{0,1:T(8,128)(2,1)S(1)}, bf16[256,512]{0,1:T(8,128)(2,1)S(1)}, u32[]{:S(2)}, u32[]{:S(2)}) collective-permute-start(bf16[256,512]{0,1:T(8,128)(2,1)S(1)} %collective-permute-done.3), channel_id=1, source_target_pairs={{0,1},{1,2},{2,3},{3,4},{4,5},{5,6},{6,7},{7,8},{8,9},{9,10},{10,1... | collective-permute-start | bytes 786440 | tf_op jit(solution)/shard_map/ppermute | solution.py:15
  18.6 0.0 collective-permute-done.6
  18.6 4.4 %collective-permute-start.7 = (bf16[256,512]{0,1:T(8,128)(2,1)S(1)}, bf16[256,512]{0,1:T(8,128)(2,1)S(1)}, u32[]{:S(2)}, u32[]{:S(2)}) collective-permute-start(bf16[256,512]{0,1:T(8,128)(2,1)S(1)} %collective-permute-done.6), channel_id=1, source_target_pairs={{0,1},{1,2},{2,3},{3,4},{4,5},{5,6},{6,7},{7,8},{8,9},{9,10},{10,1... | collective-permute-start | bytes 786440 | tf_op jit(solution)/shard_map/ppermute | solution.py:15
  23.0 3.0 %collective-permute-start = (s32[256]{0:T(256)}, s32[256]{0:T(256)S(1)}, u32[]{:S(2)}, u32[]{:S(2)}) collective-permute-start(s32[256]{0:T(256)} %param.10), channel_id=1, source_target_pairs={{0,1},{1,2},{2,3},{3,4},{4,5},{5,6},{6,7},{7,8},{8,9},{9,10},{10,1... | collective-permute-start | bytes 3080 | tf_op jit(solution)/shard_map/ppermute | solution.py:15
  26.0 1.0 collective-permute-done
  27.0 13.1 %collective-permute-start.1 = (s32[256]{0:T(256)S(1)}, s32[256]{0:T(256)S(1)}, u32[]{:S(2)}, u32[]{:S(2)}) collective-permute-start(s32[256]{0:T(256)S(1)} %collective-permute-done), channel_id=1, source_target_pairs={{0,1},{1,2},{2,3},{3,4},{4,5},{5,6},{6,7},{7,8},{8,9},{9,10},{10,1... | collective-permute-start | bytes 3080 | tf_op jit(solution)/shard_map/ppermute | solution.py:15
  40.1 0.0 collective-permute-done.4
  40.1 0.0 copy-start
  40.1 5.1 %collective-permute-start.5 = (bf16[256,512]{0,1:T(8,128)(2,1)S(1)}, bf16[256,512]{0,1:T(8,128)(2,1)}, u32[]{:S(2)}, u32[]{:S(2)}) collective-permute-start(bf16[256,512]{0,1:T(8,128)(2,1)S(1)} %collective-permute-done.4), channel_id=1, source_target_pairs={{0,1},{1,2},{2,3},{3,4},{4,5},{5,6},{6,7},{7,8},{8,9},{9,10},{10,1... | collective-permute-start | bytes 786440 | tf_op jit(solution)/shard_map/ppermute | solution.py:15
  45.2 1.3 collective-permute-start.2
  46.5 0.0 collective-permute-done.7
  46.5 6.1 %collective-permute-start.8 = (bf16[256,512]{0,1:T(8,128)(2,1)S(1)}, bf16[256,512]{0,1:T(8,128)(2,1)}, u32[]{:S(2)}, u32[]{:S(2)}) collective-permute-start(bf16[256,512]{0,1:T(8,128)(2,1)S(1)} %collective-permute-done.7), channel_id=1, source_target_pairs={{0,1},{1,2},{2,3},{3,4},{4,5},{5,6},{6,7},{7,8},{8,9},{9,10},{10,1... | collective-permute-start | bytes 786440 | tf_op jit(solution)/shard_map/ppermute | solution.py:15
  52.6 1.5 copy.6
  54.1 0.0 collective-permute-done.2
  54.1 1.2 pad_maximum_fusion
  55.3 2.1 %pad_maximum_fusion.1 = bf16[1024,512]{0,1:T(8,128)(2,1)} fusion(bf16[256,512]{0,1:T(8,128)(2,1)S(1)} %copy.9, bf16[256,512]{0,1:T(8,128)(2,1)S(1)} %collective-permute-done.6, bf16[256,512]{0,1:T(8,128)(2,1)S(1)} %collective-permute-done.7, bf16[256,512]{0,1:T(8,128)(2,1)} %collective-permute-done.8), kind=kLoop, calls=%fused_computation.25 | loop fusion | flops 4194304 | bytes 2097152 | tf_op jit(solution)/shard_map/concatenate | solution.py:59
  57.4 22.2 %while.11 = (s32[]{:T(128)}, bf16[4,256,4,128]{1,3,2,0:T(8,128)(2,1)}, bf16[4,256,4,128]{1,3,2,0:T(8,128)(2,1)S(1)}, bf16[4,1024,128]{1,2,0:T(8,128)(2,1)S(1)}, ...) while((s32[]{:T(128)}, ...), condition=%wide.region_3.4_spmd.clone, body=%wide.region_0.3_spmd.clone.sunk | while | flops 549713920 | bytes 15762541 | solution.py:46
  57.4 0.3 and_and_fusion.2
  57.7 1.0 fusion.34
  58.6 1.2 fusion.35
  59.9 2.2 %fusion.36 = bf16[1,256,4,128]{3,1,2,0:T(8,128)(2,1)S(1)} fusion(f32[256,4,1024]{2,0,1:T(8,128)S(1)} %get-tuple-element.160, f32[256,4]{0,1:T(4,128)S(1)} %get-tuple-element.161, pred[256,1024]{1,0:T(8,128)(4,1)S(1)} %and_and_fusion.2, f32[256,4]{0,1:T(4,128)S(1)} %fusion.35, bf16[4,1024,128]{1,2,0:T(8,128)(2,1)} %get-tuple-element.188, ...), kind=kOutput, calls=%fused_computation.10.clone.1 | convolution fusion | flops 272891904 | bytes 4989440 | tf_op jit(solution)/shard_map/while/body/eval_jaxpr/ths,sd->thd/dot_general | solution.py:29
  62.1 0.1 copy.21
  62.2 0.7 constant_dynamic-update-slice_fusion.2
  62.9 0.3 and_and_fusion.2
  63.3 1.0 fusion.34
  64.2 1.2 fusion.35
  65.4 2.2 %fusion.36 = bf16[1,256,4,128]{3,1,2,0:T(8,128)(2,1)S(1)} fusion(f32[256,4,1024]{2,0,1:T(8,128)S(1)} %get-tuple-element.160, f32[256,4]{0,1:T(4,128)S(1)} %get-tuple-element.161, pred[256,1024]{1,0:T(8,128)(4,1)S(1)} %and_and_fusion.2, f32[256,4]{0,1:T(4,128)S(1)} %fusion.35, bf16[4,1024,128]{1,2,0:T(8,128)(2,1)} %get-tuple-element.188, ...), kind=kOutput, calls=%fused_computation.10.clone.1 | convolution fusion | flops 272891904 | bytes 4989440 | tf_op jit(solution)/shard_map/while/body/eval_jaxpr/ths,sd->thd/dot_general | solution.py:29
  67.6 0.1 copy.21
  67.8 0.7 constant_dynamic-update-slice_fusion.2
  68.5 0.3 and_and_fusion.2
  68.8 1.0 fusion.34
  69.8 1.2 fusion.35
  71.0 2.2 %fusion.36 = bf16[1,256,4,128]{3,1,2,0:T(8,128)(2,1)S(1)} fusion(f32[256,4,1024]{2,0,1:T(8,128)S(1)} %get-tuple-element.160, f32[256,4]{0,1:T(4,128)S(1)} %get-tuple-element.161, pred[256,1024]{1,0:T(8,128)(4,1)S(1)} %and_and_fusion.2, f32[256,4]{0,1:T(4,128)S(1)} %fusion.35, bf16[4,1024,128]{1,2,0:T(8,128)(2,1)} %get-tuple-element.188, ...), kind=kOutput, calls=%fused_computation.10.clone.1 | convolution fusion | flops 272891904 | bytes 4989440 | tf_op jit(solution)/shard_map/while/body/eval_jaxpr/ths,sd->thd/dot_general | solution.py:29
  73.2 0.1 copy.21
  73.4 0.7 constant_dynamic-update-slice_fusion.2
  74.1 0.3 and_and_fusion.2
  74.4 0.9 fusion.34
  75.3 1.2 fusion.35
  76.5 2.2 %fusion.36 = bf16[1,256,4,128]{3,1,2,0:T(8,128)(2,1)S(1)} fusion(f32[256,4,1024]{2,0,1:T(8,128)S(1)} %get-tuple-element.160, f32[256,4]{0,1:T(4,128)S(1)} %get-tuple-element.161, pred[256,1024]{1,0:T(8,128)(4,1)S(1)} %and_and_fusion.2, f32[256,4]{0,1:T(4,128)S(1)} %fusion.35, bf16[4,1024,128]{1,2,0:T(8,128)(2,1)} %get-tuple-element.188, ...), kind=kOutput, calls=%fused_computation.10.clone.1 | convolution fusion | flops 272891904 | bytes 4989440 | tf_op jit(solution)/shard_map/while/body/eval_jaxpr/ths,sd->thd/dot_general | solution.py:29
  78.8 0.1 copy.21
  78.9 0.7 constant_dynamic-update-slice_fusion.2
  79.6 68.0 %all-gather.2.cloned.1.call-done = bf16[2048,4096]{1,0:T(8,128)(2,1)} async-done(((bf16[128,4096]{1,0:T(8,128)(2,1)}), bf16[2048,4096]{1,0:T(8,128)(2,1)}) %all-gather.2.cloned.1.call-update) | async-done | bytes 16777232 | tf_op jit(solution)/shard_map/all_gather | solution.py:72
  147.6 12.0 %convolution_convert_fusion = bf16[256,4096]{1,0:T(8,128)(2,1)} fusion(bf16[256,2048]{0,1:T(8,128)(2,1)} %bitcast.44, bf16[2048,4096]{1,0:T(8,128)(2,1)} %all-gather.2.cloned.1.call-done), kind=kOutput, calls=%fused_computation.23 | convolution fusion | flops 4296015872 | bytes 19922944 | tf_op jit(solution)/shard_map/dot_general | solution.py:70
  (13 shorter events, 0.0 us)
Async XLA Ops:
  6.5 47.5 %copy-start.1 = (s32[256]{0:T(256)S(1)}, s32[256]{0:T(256)}, u32[]{:S(2)}) copy-start(s32[256]{0:T(256)} %param.10) | copy-start | bytes 3076
  6.5 141.1 %all-gather.2.cloned.1.call-start = ((), (), s32[]{:S(2)}) async-start(), calls=%async_computation | async-start | bytes 17825792 | tf_op jit(solution)/shard_map/all_gather | solution.py:72
  8.3 8.0 %collective-permute-start.3 = (bf16[256,512]{0,1:T(8,128)(2,1)S(1)}, bf16[256,512]{0,1:T(8,128)(2,1)S(1)}, u32[]{:S(2)}, u32[]{:S(2)}) collective-permute-start(bf16[256,512]{0,1:T(8,128)(2,1)S(1)} %copy.7), channel_id=1, source_target_pairs={{0,1},{1,2},{2,3},{3,4},{4,5},{5,6},{6,7},{7,8},{8,9},{9,10},{10,1... | collective-permute-start | bytes 786440 | tf_op jit(solution)/shard_map/ppermute | solution.py:15
  11.8 6.7 %collective-permute-start.6 = (bf16[256,512]{0,1:T(8,128)(2,1)S(1)}, bf16[256,512]{0,1:T(8,128)(2,1)S(1)}, u32[]{:S(2)}, u32[]{:S(2)}) collective-permute-start(bf16[256,512]{0,1:T(8,128)(2,1)S(1)} %copy.9), channel_id=1, source_target_pairs={{0,1},{1,2},{2,3},{3,4},{4,5},{5,6},{6,7},{7,8},{8,9},{9,10},{10,1... | collective-permute-start | bytes 786440 | tf_op jit(solution)/shard_map/ppermute | solution.py:15
  16.4 23.7 %collective-permute-start.4 = (bf16[256,512]{0,1:T(8,128)(2,1)S(1)}, bf16[256,512]{0,1:T(8,128)(2,1)S(1)}, u32[]{:S(2)}, u32[]{:S(2)}) collective-permute-start(bf16[256,512]{0,1:T(8,128)(2,1)S(1)} %collective-permute-done.3), channel_id=1, source_target_pairs={{0,1},{1,2},{2,3},{3,4},{4,5},{5,6},{6,7},{7,8},{8,9},{9,10},{10,1... | collective-permute-start | bytes 786440 | tf_op jit(solution)/shard_map/ppermute | solution.py:15
  18.6 28.0 %collective-permute-start.7 = (bf16[256,512]{0,1:T(8,128)(2,1)S(1)}, bf16[256,512]{0,1:T(8,128)(2,1)S(1)}, u32[]{:S(2)}, u32[]{:S(2)}) collective-permute-start(bf16[256,512]{0,1:T(8,128)(2,1)S(1)} %collective-permute-done.6), channel_id=1, source_target_pairs={{0,1},{1,2},{2,3},{3,4},{4,5},{5,6},{6,7},{7,8},{8,9},{9,10},{10,1... | collective-permute-start | bytes 786440 | tf_op jit(solution)/shard_map/ppermute | solution.py:15
  23.0 4.0 %collective-permute-start = (s32[256]{0:T(256)}, s32[256]{0:T(256)S(1)}, u32[]{:S(2)}, u32[]{:S(2)}) collective-permute-start(s32[256]{0:T(256)} %param.10), channel_id=1, source_target_pairs={{0,1},{1,2},{2,3},{3,4},{4,5},{5,6},{6,7},{7,8},{8,9},{9,10},{10,1... | collective-permute-start | bytes 3080 | tf_op jit(solution)/shard_map/ppermute | solution.py:15
  27.0 18.2 %collective-permute-start.1 = (s32[256]{0:T(256)S(1)}, s32[256]{0:T(256)S(1)}, u32[]{:S(2)}, u32[]{:S(2)}) collective-permute-start(s32[256]{0:T(256)S(1)} %collective-permute-done), channel_id=1, source_target_pairs={{0,1},{1,2},{2,3},{3,4},{4,5},{5,6},{6,7},{7,8},{8,9},{9,10},{10,1... | collective-permute-start | bytes 3080 | tf_op jit(solution)/shard_map/ppermute | solution.py:15
  40.1 14.0 %copy-start = (bf16[256,512]{0,1:T(8,128)(2,1)}, bf16[256,512]{0,1:T(8,128)(2,1)S(1)}, u32[]{:S(2)}) copy-start(bf16[256,512]{0,1:T(8,128)(2,1)S(1)} %collective-permute-done.4) | copy-start | bytes 786436
  40.1 14.0 %collective-permute-start.5 = (bf16[256,512]{0,1:T(8,128)(2,1)S(1)}, bf16[256,512]{0,1:T(8,128)(2,1)}, u32[]{:S(2)}, u32[]{:S(2)}) collective-permute-start(bf16[256,512]{0,1:T(8,128)(2,1)S(1)} %collective-permute-done.4), channel_id=1, source_target_pairs={{0,1},{1,2},{2,3},{3,4},{4,5},{5,6},{6,7},{7,8},{8,9},{9,10},{10,1... | collective-permute-start | bytes 786440 | tf_op jit(solution)/shard_map/ppermute | solution.py:15
  45.2 8.9 %collective-permute-start.2 = (s32[256]{0:T(256)S(1)}, s32[256]{0:T(256)S(1)}, u32[]{:S(2)}, u32[]{:S(2)}) collective-permute-start(s32[256]{0:T(256)S(1)} %collective-permute-done.1), channel_id=1, source_target_pairs={{0,1},{1,2},{2,3},{3,4},{4,5},{5,6},{6,7},{7,8},{8,9},{9,10},{10,1... | collective-permute-start | bytes 3080 | tf_op jit(solution)/shard_map/ppermute | solution.py:15
  46.5 8.8 %collective-permute-start.8 = (bf16[256,512]{0,1:T(8,128)(2,1)S(1)}, bf16[256,512]{0,1:T(8,128)(2,1)}, u32[]{:S(2)}, u32[]{:S(2)}) collective-permute-start(bf16[256,512]{0,1:T(8,128)(2,1)S(1)} %collective-permute-done.7), channel_id=1, source_target_pairs={{0,1},{1,2},{2,3},{3,4},{4,5},{5,6},{6,7},{7,8},{8,9},{9,10},{10,1... | collective-permute-start | bytes 786440 | tf_op jit(solution)/shard_map/ppermute | solution.py:15
Sparse Core Ops, SparseCore 0:
  9.5 138.0 all-gather.1
where the time goes:
time: 167 us; the launch traced here: 166 us
  waiting for transfers between devices  69.7 us (42%)
  starting transfers between devices  42 us (25%)
  matrix products  24.6 us (15%)
  between operations  13.6 us (8%)
  other arithmetic  9.34 us (6%)
  local copies, waits for them, and re-layouts  7.13 us (4%)
    all_gather x1, waiting for transfers between devices, body(): lax.all_gather(out_weight, 'seq', axis=0, tiled=True)  68 us
    ppermute x9, starting transfers between devices, shifted(): return lax.ppermute(block, axis, route)  42 us
    dot_general x1, matrix products, body(): jnp.dot(attention, lax.all_gather(out_weight, 'seq', axis=0, tiled=True),...  12 us
    dot_general x4, matrix products, one_head(): jnp.einsum('ths,sd->thd', probabilities, value_head, preferred_element_ty...  8.79 us
    reduce_sum x4, other arithmetic, one_head(): weight_sum = jnp.sum(weights, axis=-1, keepdims=True)  4.86 us
    dot_general x4, matrix products, one_head(): jnp.einsum('thd,sd->ths', query_group, key_head, preferred_element_type=j...  3.81 us
    unnamed x7, local copies, waits for them, and re-layouts  3.65 us
    dynamic_update_slice x8, local copies, waits for them, and re-layouts, attend(): head_outputs = lax.map(per_group, (query_heads, key_heads, value_heads))  3.48 us
  transfers between devices with their start and end apart: 10, of which 2 were waited for; matrix products, arithmetic and copies ran while one was open for 17% of the time, Pallas kernels for 0%

commit v1 on v0

v1 whole, which is shorter than its diff:
```python
import functools
import math

import jax
import jax.numpy as jnp
from jax import lax
from jax.experimental import pallas as pl
from jax.experimental.pallas import tpu as pltpu
from jax.sharding import PartitionSpec as P

HEADS = 16
KV_HEADS = 4
HEAD = 128
SPAN = 4
CORES = 2
UP_A, DOWN_A, UP_B, DOWN_B, ACROSS, SIBLING = range(6)


def grid_of(n):
    chips = n // CORES
    b = max(d for d in range(1, chips + 1) if chips % d == 0 and d * d <= chips)
    return chips // b, b


def kernel(n, A, B, wx, tile,
           q_ref, k_ref, v_ref, seg_row_ref, seg_col_ref, w_ref, out_ref,
           W, kwin, vwin, swin, bias, att,
           send, recv, kv_send, kv_recv):
    rows = q_ref.shape[0]
    depth = w_ref.shape[0]
    width = w_ref.shape[1]
    g = lax.axis_index("groups")
    i = lax.axis_index("seq")
    c = lax.rem(i, CORES)
    chip = i // CORES
    b = lax.rem(chip, B)
    a = chip // B

    def index(a_, b_, c_):
        return (a_ * B + b_) * CORES + c_

    widths = (wx, width - 2 * wx, wx)
    starts = (g * wx, 2 * wx, (1 - g) * wx)
    number = (g, 2, 1 - g)

    def move(p, s, way, device):
        view = W.at[pl.ds(pl.multiple_of(s * depth, depth), depth),
                    pl.ds(pl.multiple_of(starts[p], 128), widths[p])]
        return pltpu.make_async_remote_copy(
            src_ref=view, dst_ref=view,
            send_sem=send.at[way, p, s], recv_sem=recv.at[number[p], s],
            device_id=device, device_id_type=pl.DeviceIdType.MESH)

    def act(copy, mode):
        if mode == "start":
            copy.start()
        else:
            copy.wait_send()

    up_a = (g, index(a + 1, b, c))
    down_a = (g, index(a - 1, b, c))
    up_b = (g, index(a, b + 1, c))
    down_b = (g, index(a, b - 1, c))
    across = (1 - g, i)
    sibling = (g, index(a, b, 1 - c))

    def along_b(p, s, mode):
        pl.when(b + 1 < B)(lambda: act(move(p, s, UP_B, up_b), mode))
        pl.when(b > 0)(lambda: act(move(p, s, DOWN_B, down_b), mode))

    def arrive(p, s, mode):
        if mode == "start":
            move(p, s, SIBLING, sibling).wait_recv()

    def own(mode):
        for p in (0, 1):
            pl.when(a + 1 < A)(lambda: act(move(p, i, UP_A, up_a), mode))
            pl.when(a > 0)(lambda: act(move(p, i, DOWN_A, down_a), mode))
            along_b(p, i, mode)
        for p in (0, 1, 2):
            act(move(p, i, SIBLING, sibling), mode)

    def from_a(p, t, mode):
        def take(a_, way, device, more):
            s = index(a_, b, c)
            arrive(p, s, mode)
            pl.when(more)(lambda: act(move(p, s, way, device), mode))
            along_b(p, s, mode)
            if p == 0:
                act(move(p, s, ACROSS, across), mode)
            act(move(p, s, SIBLING, sibling), mode)

        pl.when(a - t >= 0)(lambda: take(a - t, UP_A, up_a, a + 1 < A))
        pl.when(a + t < A)(lambda: take(a + t, DOWN_A, down_a, a > 0))

    def from_b(p, t, mode):
        def take(a_, b_, way, device, more):
            s = index(a_, b_, c)
            arrive(p, s, mode)
            pl.when(more)(lambda: act(move(p, s, way, device), mode))
            if p == 0:
                act(move(p, s, ACROSS, across), mode)
            act(move(p, s, SIBLING, sibling), mode)

        def column(a_):
            def step(u, carry):
                pl.when(b - u >= 0)(lambda: take(a_, b - u, UP_B, up_b, b + 1 < B))
                pl.when(b + u < B)(lambda: take(a_, b + u, DOWN_B, down_b, b > 0))
                return carry

            lax.fori_loop(1, B, step, 0)

        if t == 0:
            column(a)
        else:
            pl.when(a - t >= 0)(lambda: column(a - t))
            pl.when(a + t < A)(lambda: column(a + t))

    def from_across(t, mode):
        def column(a_):
            def step(b_, carry):
                s = index(a_, b_, c)

                @pl.when(s != i)
                def _():
                    arrive(2, s, mode)
                    act(move(2, s, SIBLING, sibling), mode)

                return carry

            lax.fori_loop(0, B, step, 0)

        if t == 0:
            column(a)
        else:
            pl.when(a - t >= 0)(lambda: column(a - t))
            pl.when(a + t < A)(lambda: column(a + t))

    def kv_copies(d):
        to = (g, lax.rem(i + d, n))
        mine, theirs = SPAN - 1, SPAN - 1 - d
        return [
            pltpu.make_async_remote_copy(
                src_ref=ref.at[mine], dst_ref=ref.at[theirs],
                send_sem=kv_send.at[d - 1, m], recv_sem=kv_recv.at[d - 1, m],
                device_id=to, device_id_type=pl.DeviceIdType.MESH)
            for m, ref in enumerate((kwin, vwin, swin))]

    barrier = pltpu.get_barrier_semaphore()

    def greet(device):
        pl.semaphore_signal(barrier, inc=1, device_id=device,
                            device_id_type=pl.DeviceIdType.MESH)

    pl.when(a + 1 < A)(lambda: greet(up_a))
    pl.when(a > 0)(lambda: greet(down_a))
    pl.when(b + 1 < B)(lambda: greet(up_b))
    pl.when(b > 0)(lambda: greet(down_b))
    greet(across)
    greet(sibling)
    for d in range(1, SPAN):
        greet((g, lax.rem(i + d, n)))
        greet((g, lax.rem(i + n - d, n)))
    W[pl.ds(pl.multiple_of(i * depth, depth), depth), :] = w_ref[...]
    kwin[SPAN - 1] = k_ref[...]
    vwin[SPAN - 1] = v_ref[...]
    swin[SPAN - 1] = seg_row_ref[...]
    expected = (2 + 2 * (SPAN - 1)
                + jnp.where(a + 1 < A, 1, 0) + jnp.where(a > 0, 1, 0)
                + jnp.where(b + 1 < B, 1, 0) + jnp.where(b > 0, 1, 0))
    pl.semaphore_wait(barrier, expected)

    for d in range(1, SPAN):
        for copy in kv_copies(d):
            copy.start()
    own("start")
    for d in range(1, SPAN):
        for copy in kv_copies(d):
            copy.wait_recv()

    for j in range(SPAN):
        row = lax.broadcasted_iota(jnp.int32, (rows, rows), 0)
        col = lax.broadcasted_iota(jnp.int32, (rows, rows), 1) + (j - SPAN + 1) * rows
        live = (seg_col_ref[:, 0:1] == swin[j, 0:1, :]) & (col <= row) & (col + i * rows >= 0)
        bias[:, j * rows:(j + 1) * rows] = jnp.where(live, 0.0, -jnp.inf)

    factor = HEAD ** -0.5 * math.log2(math.e)
    group = HEADS // KV_HEADS

    def attend(kv):
        lanes = slice(kv * HEAD, (kv + 1) * HEAD)
        keys = jnp.concatenate([kwin[j, :, lanes] for j in range(SPAN)], axis=0)
        vals = jnp.concatenate([vwin[j, :, lanes] for j in range(SPAN)], axis=0)
        for m in range(group):
            h = kv * group + m
            q = q_ref[:, h * HEAD:(h + 1) * HEAD]
            scores = lax.dot_general(q, keys, (((1,), (1,)), ((), ())),
                                     preferred_element_type=jnp.float32)
            scores = scores * factor + bias[...]
            top = jnp.max(scores, axis=-1, keepdims=True)
            weights = jnp.exp2(scores - top)
            total = jnp.sum(weights, axis=-1, keepdims=True)
            mix = jnp.dot(weights.astype(jnp.bfloat16), vals,
                          preferred_element_type=jnp.float32)
            att[:, h * HEAD:(h + 1) * HEAD] = (mix / total).astype(jnp.bfloat16)

    done = 0
    for t in range(A):
        if t > 0:
            from_a(0, t, "start")
        from_b(0, t, "start")
        if t > 0:
            from_a(1, t, "start")
        from_b(1, t, "start")
        if t > 1:
            from_across(t - 2, "start")
        if done < KV_HEADS:
            attend(done)
            done += 1
    for kv in range(done, KV_HEADS):
        attend(kv)

    def project(p):
        def landed(m, carry):
            move(p, m * CORES + 1 - c, SIBLING, sibling).wait_recv()
            return carry

        lax.fori_loop(0, n // CORES, landed, 0)

        def one(m, carry):
            lanes = pl.ds(pl.multiple_of(starts[p] + m * tile, 128), tile)
            out_ref[:, lanes] = jnp.dot(
                att[...], W[:, lanes], preferred_element_type=jnp.float32
            ).astype(out_ref.dtype)
            return carry

        lax.fori_loop(0, widths[p] // tile, one, 0)

    project(0)
    for t in range(max(A - 2, 0), A):
        from_across(t, "start")
    project(1)
    project(2)

    own("wait")
    for t in range(A):
        for p in (0, 1):
            if t > 0:
                from_a(p, t, "wait")
            from_b(p, t, "wait")
        from_across(t, "wait")
    for d in range(1, SPAN):
        for copy in kv_copies(d):
            copy.wait_send()


def body(queries, keys, values, segment, out_weight):
    rows, q_width = queries.shape
    kv_width = keys.shape[1]
    n = lax.axis_size("seq")
    width = out_weight.shape[1]
    A, B = grid_of(n)
    tile = math.gcd(width, 512)
    wx = width * 3 // 8 // tile * tile
    seg_row = jnp.broadcast_to(segment[None, :], (8, rows))
    seg_col = jnp.broadcast_to(segment[:, None], (rows, 128))
    vmem = pl.BlockSpec(memory_space=pltpu.VMEM)
    window = rows * SPAN
    return pl.pallas_call(
        functools.partial(kernel, n, A, B, wx, tile),
        out_shape=jax.ShapeDtypeStruct((rows, width), jnp.bfloat16),
        in_specs=[vmem] * 6,
        out_specs=vmem,
        scratch_shapes=[
            pltpu.VMEM((out_weight.shape[0] * n, width), jnp.bfloat16),
            pltpu.VMEM((SPAN, rows, kv_width), jnp.bfloat16),
            pltpu.VMEM((SPAN, rows, kv_width), jnp.bfloat16),
            pltpu.VMEM((SPAN, 8, rows), jnp.int32),
            pltpu.VMEM((rows, window), jnp.float32),
            pltpu.VMEM((rows, q_width), jnp.bfloat16),
            pltpu.SemaphoreType.DMA((6, 3, n)),
            pltpu.SemaphoreType.DMA((3, n)),
            pltpu.SemaphoreType.DMA((SPAN - 1, 3)),
            pltpu.SemaphoreType.DMA((SPAN - 1, 3)),
        ],
        compiler_params=pltpu.CompilerParams(
            collective_id=0, has_side_effects=True, vmem_limit_bytes=56 * 2**20),
        cost_estimate=pl.CostEstimate(
            flops=2 * rows * q_width * (2 * window + width),
            bytes_accessed=4 * rows * width, transcendentals=rows * window * HEADS),
    )(queries, keys, values, seg_row, seg_col, out_weight)


def solution(mesh):
    in_specs = (
        P(("groups", "seq"), None),
        P(("groups", "seq"), None),
        P(("groups", "seq"), None),
        P(("groups", "seq")),
        P("seq", None),
    )
    out_specs = P(("groups", "seq"), None)
    return jax.shard_map(body, mesh=mesh, in_specs=in_specs, out_specs=out_specs, check_vma=False)
```

time: 167 us -> 127 us (0.76)
  Pallas kernels: 0 us -> 119 us
  waiting for transfers between devices: 69.7 us -> 0 us
  starting transfers between devices: 42 us -> 0 us
  matrix products: 24.6 us -> 0 us
  between operations: 13.6 us -> 0.01 us
  other arithmetic: 9.34 us -> 0 us
    pallas_call x0 -> x1, Pallas kernels: none -> 119 us  [body(): pl.pallas_call(functools.partial(kernel, n, A, B, wx, tile), out_shape=ja...]
    all_gather x1 -> x0, waiting for transfers between devices: 68 us -> none  [body(): lax.all_gather(out_weight, 'seq', axis=0, tiled=True)]
    ppermute x9 -> x0, starting transfers between devices: 42 us -> none  [shifted(): return lax.ppermute(block, axis, route)]
    dot_general x9 -> x0, matrix products: 24.6 us -> none  [the longest x1 12 us: body(): jnp.dot(attention, lax.all_gather(out_weight, 'seq', axis=0, tiled=True),...]
    reduce_sum x4 -> x0, other arithmetic: 4.86 us -> none  [one_head(): weight_sum = jnp.sum(weights, axis=-1, keepdims=True)]
    dynamic_update_slice x8 -> x0, local copies, waits for them, and re-layouts: 3.48 us -> none  [attend(): head_outputs = lax.map(per_group, (query_heads, key_heads, value_heads))]
    concatenate x3 -> x0, other arithmetic: 3.23 us -> none  [body(): jnp.concatenate([arrival[member] for arrival in collected], axis=0)]
    broadcast_in_dim x0 -> x2, local copies, waits for them, and re-layouts: none -> 2.71 us  [the longest x1 1.43 us: body(): seg_col = jnp.broadcast_to(segment[:, None], (rows, 128))]
  transfers between devices with their start and end apart: 10 -> 0, of which waited for: 2 -> 0; matrix products, arithmetic and copies ran while one was open for 17% -> 0% of each run, Pallas kernels for 0% -> 0%
where the time goes in v1:
time: 127 us; the launch traced here: 125 us
  Pallas kernels  119 us (94%)
  local copies, waits for them, and re-layouts  5.84 us (5%)
    pallas_call x1, Pallas kernels, body(): pl.pallas_call(functools.partial(kernel, n, A, B, wx, tile), out_shape=ja...  119 us
    unnamed x1, local copies, waits for them, and re-layouts  3.13 us

profile of v1, /device:TPU:0, one launch (start us, length us, event | category | flops | bytes accessed | tf_op | source)
XLA Modules:
  0.0 125.2 jit_solution(4534308453244231559)
XLA Ops:
  0.0 1.3 %broadcast_in_dim.4.seg_row_ref = s32[8,256]{1,0:T(8,128)} broadcast(s32[256]{0:T(256)} %param.8), dimensions={1} | broadcast | bytes 9216 | tf_op jit(solution)/shard_map/broadcast_in_dim | solution.py:265
  1.3 1.4 %broadcast_in_dim.5.seg_col_ref = s32[256,128]{1,0:T(8,128)} broadcast(s32[256]{0:T(256)} %param.8), dimensions={0} | broadcast | bytes 132096 | tf_op jit(solution)/shard_map/broadcast_in_dim | solution.py:266
  2.7 119.4 %shard_map.55 = bf16[256,4096]{1,0:T(8,128)(2,1)} custom-call(bf16[256,2048]{1,0:T(8,128)(2,1)} %q_ref.1, bf16[256,512]{1,0:T(8,128)(2,1)} %k_ref.1, bf16[256,512]{1,0:T(8,128)(2,1)} %v_ref.1, s32[8,256]{1,0:T(8,128)} %broadcast_in_dim.4.seg_row_ref, s32[256,128]{1,0:T(8,128)} %broadcast_in_dim.5.seg_col_ref, bf16[128,4096]{1,0:T(8,128)(2,1)} %w_ref.1), custom_call_target="tpu_custom_call" | custom-call | flops 6442450944 | bytes 4194304 | tf_op jit(solution)/shard_map/pallas_call | solution.py:269
  122.1 3.1 %copy.7 = bf16[256,4096]{1,0:T(8,128)(2,1)} copy(bf16[256,4096]{1,0:T(8,128)(2,1)} %shard_map.55) | data formatting | bytes 4194304

commit v2 on v1

--- a/solution.py
+++ b/solution.py
@@ -22,7 +22,7 @@
     return chips // b, b
 
 
-def kernel(n, A, B, wx, tile,
+def kernel(n, A, B, wx, cuts, tile,
            q_ref, k_ref, v_ref, seg_row_ref, seg_col_ref, w_ref, out_ref,
            W, kwin, vwin, swin, bias, att,
            send, recv, kv_send, kv_recv):
@@ -39,9 +39,16 @@
     def index(a_, b_, c_):
         return (a_ * B + b_) * CORES + c_
 
-    widths = (wx, width - 2 * wx, wx)
-    starts = (g * wx, 2 * wx, (1 - g) * wx)
-    number = (g, 2, 1 - g)
+    part = wx // cuts
+    rest = width - 2 * wx
+    MINE = tuple(range(cuts))
+    BOTH = (cuts,)
+    THEIRS = tuple(range(cuts + 1, 2 * cuts + 1))
+    widths = (part,) * cuts + (rest,) + (part,) * cuts
+    starts = (tuple(g * wx + j * part for j in range(cuts)) + (2 * wx,)
+              + tuple((1 - g) * wx + j * part for j in range(cuts)))
+    number = (tuple(g * cuts + j for j in range(cuts)) + (2 * cuts,)
+              + tuple((1 - g) * cuts + j for j in range(cuts)))
 
     def move(p, s, way, device):
         view = W.at[pl.ds(pl.multiple_of(s * depth, depth), depth),
@@ -72,12 +79,11 @@
         if mode == "start":
             move(p, s, SIBLING, sibling).wait_recv()
 
-    def own(mode):
-        for p in (0, 1):
+    def own(pieces, mode):
+        for p in pieces:
             pl.when(a + 1 < A)(lambda: act(move(p, i, UP_A, up_a), mode))
             pl.when(a > 0)(lambda: act(move(p, i, DOWN_A, down_a), mode))
             along_b(p, i, mode)
-        for p in (0, 1, 2):
             act(move(p, i, SIBLING, sibling), mode)
 
     def from_a(p, t, mode):
@@ -86,7 +92,7 @@
             arrive(p, s, mode)
             pl.when(more)(lambda: act(move(p, s, way, device), mode))
             along_b(p, s, mode)
-            if p == 0:
+            if p in MINE:
                 act(move(p, s, ACROSS, across), mode)
             act(move(p, s, SIBLING, sibling), mode)
 
@@ -98,7 +104,7 @@
             s = index(a_, b_, c)
             arrive(p, s, mode)
             pl.when(more)(lambda: act(move(p, s, way, device), mode))
-            if p == 0:
+            if p in MINE:
                 act(move(p, s, ACROSS, across), mode)
             act(move(p, s, SIBLING, sibling), mode)
 
@@ -116,15 +122,15 @@
             pl.when(a - t >= 0)(lambda: column(a - t))
             pl.when(a + t < A)(lambda: column(a + t))
 
-    def from_across(t, mode):
+    def from_across(p, t, mode):
         def column(a_):
             def step(b_, carry):
                 s = index(a_, b_, c)
 
                 @pl.when(s != i)
                 def _():
-                    arrive(2, s, mode)
-                    act(move(2, s, SIBLING, sibling), mode)
+                    arrive(p, s, mode)
+                    act(move(p, s, SIBLING, sibling), mode)
 
                 return carry
 
@@ -136,13 +142,17 @@
             pl.when(a - t >= 0)(lambda: column(a - t))
             pl.when(a + t < A)(lambda: column(a + t))
 
-    def kv_copies(d):
-        to = (g, lax.rem(i + d, n))
-        mine, theirs = SPAN - 1, SPAN - 1 - d
+    last = SPAN - 1
+    routes = ((last, 1, (g, lax.rem(i + 2, n))),
+              (1, 2 * c, sibling),
+              (last, 2 - 2 * c, (g, lax.rem(i + 1 + 2 * c, n))))
+
+    def kv_copies(way):
+        mine, theirs, to = routes[way]
         return [
             pltpu.make_async_remote_copy(
                 src_ref=ref.at[mine], dst_ref=ref.at[theirs],
-                send_sem=kv_send.at[d - 1, m], recv_sem=kv_recv.at[d - 1, m],
+                send_sem=kv_send.at[way, m], recv_sem=kv_recv.at[theirs, m],
                 device_id=to, device_id_type=pl.DeviceIdType.MESH)
             for m, ref in enumerate((kwin, vwin, swin))]
 
@@ -170,19 +180,28 @@
                 + jnp.where(b + 1 < B, 1, 0) + jnp.where(b > 0, 1, 0))
     pl.semaphore_wait(barrier, expected)
 
-    for d in range(1, SPAN):
-        for copy in kv_copies(d):
+    own(MINE, "start")
+    for way in (0, 2):
+        for copy in kv_copies(way):
             copy.start()
-    own("start")
-    for d in range(1, SPAN):
-        for copy in kv_copies(d):
-            copy.wait_recv()
-
-    for j in range(SPAN):
-        row = lax.broadcasted_iota(jnp.int32, (rows, rows), 0)
-        col = lax.broadcasted_iota(jnp.int32, (rows, rows), 1) + (j - SPAN + 1) * rows
-        live = (seg_col_ref[:, 0:1] == swin[j, 0:1, :]) & (col <= row) & (col + i * rows >= 0)
-        bias[:, j * rows:(j + 1) * rows] = jnp.where(live, 0.0, -jnp.inf)
+    own(BOTH, "start")
+    for p in THEIRS:
+        move(p, i, SIBLING, sibling).start()
+
+    def slot(j):
+        return [
+            pltpu.make_async_remote_copy(
+                src_ref=ref.at[last], dst_ref=ref.at[j],
+                send_sem=kv_send.at[0, m], recv_sem=kv_recv.at[j, m],
+                device_id=sibling, device_id_type=pl.DeviceIdType.MESH)
+            for m, ref in enumerate((kwin, vwin, swin))]
+
+    def mask():
+        for j in range(SPAN):
+            row = lax.broadcasted_iota(jnp.int32, (rows, rows), 0)
+            col = lax.broadcasted_iota(jnp.int32, (rows, rows), 1) + (j - SPAN + 1) * rows
+            live = (seg_col_ref[:, 0:1] == swin[j, 0:1, :]) & (col <= row) & (col + i * rows >= 0)
+            bias[:, j * rows:(j + 1) * rows] = jnp.where(live, 0.0, -jnp.inf)
 
     factor = HEAD ** -0.5 * math.log2(math.e)
     group = HEADS // KV_HEADS
@@ -206,17 +225,26 @@
 
     done = 0
     for t in range(A):
+        for p in MINE + BOTH:
+            if t > 0:
+                from_a(p, t, "start")
+            from_b(p, t, "start")
+        if t == 0:
+            for copy in slot(1):
+                copy.wait_recv()
+            for copy in kv_copies(1):
+                copy.start()
+        if t == 1:
+            for j in (0, 2):
+                for copy in slot(j):
+                    copy.wait_recv()
+            mask()
         if t > 0:
-            from_a(0, t, "start")
-        from_b(0, t, "start")
-        if t > 0:
-            from_a(1, t, "start")
-        from_b(1, t, "start")
-        if t > 1:
-            from_across(t - 2, "start")
-        if done < KV_HEADS:
-            attend(done)
-            done += 1
+            for p in THEIRS:
+                from_across(p, t - 1, "start")
+            if done < KV_HEADS:
+                attend(done)
+                done += 1
     for kv in range(done, KV_HEADS):
         attend(kv)
 
@@ -236,21 +264,25 @@
 
         lax.fori_loop(0, widths[p] // tile, one, 0)
 
-    project(0)
-    for t in range(max(A - 2, 0), A):
-        from_across(t, "start")
-    project(1)
-    project(2)
-
-    own("wait")
+    for p in MINE:
+        project(p)
+    for p in THEIRS:
+        from_across(p, A - 1, "start")
+    for p in BOTH + THEIRS:
+        project(p)
+
+    own(MINE + BOTH, "wait")
+    for p in THEIRS:
+        move(p, i, SIBLING, sibling).wait_send()
     for t in range(A):
-        for p in (0, 1):
+        for p in MINE + BOTH:
             if t > 0:
                 from_a(p, t, "wait")
             from_b(p, t, "wait")
-        from_across(t, "wait")
-    for d in range(1, SPAN):
-        for copy in kv_copies(d):
+        for p in THEIRS:
+            from_across(p, t, "wait")
+    for way in range(3):
+        for copy in kv_copies(way):
             copy.wait_send()
 
 
@@ -261,13 +293,14 @@
     width = out_weight.shape[1]
     A, B = grid_of(n)
     tile = math.gcd(width, 512)
-    wx = width * 3 // 8 // tile * tile
+    cuts = 1
+    wx = width * 3 // 8 // (cuts * tile) * (cuts * tile)
     seg_row = jnp.broadcast_to(segment[None, :], (8, rows))
     seg_col = jnp.broadcast_to(segment[:, None], (rows, 128))
     vmem = pl.BlockSpec(memory_space=pltpu.VMEM)
     window = rows * SPAN
     return pl.pallas_call(
-        functools.partial(kernel, n, A, B, wx, tile),
+        functools.partial(kernel, n, A, B, wx, cuts, tile),
         out_shape=jax.ShapeDtypeStruct((rows, width), jnp.bfloat16),
         in_specs=[vmem] * 6,
         out_specs=vmem,
@@ -278,8 +311,8 @@
             pltpu.VMEM((SPAN, 8, rows), jnp.int32),
             pltpu.VMEM((rows, window), jnp.float32),
             pltpu.VMEM((rows, q_width), jnp.bfloat16),
-            pltpu.SemaphoreType.DMA((6, 3, n)),
-            pltpu.SemaphoreType.DMA((3, n)),
+            pltpu.SemaphoreType.DMA((6, 2 * cuts + 1, n)),
+            pltpu.SemaphoreType.DMA((2 * cuts + 1, n)),
             pltpu.SemaphoreType.DMA((SPAN - 1, 3)),
             pltpu.SemaphoreType.DMA((SPAN - 1, 3)),
         ],

time: 127 us -> 111 us (0.87); the launches traced: 125 us -> 111 us
  Pallas kernels: 119 us -> 105 us
    pallas_call x1, Pallas kernels: 119 us -> 105 us  [body(): pl.pallas_call(functools.partial(kernel, n, A, B, wx, cuts, tile), out_sh...]
where the time goes in v2:
time: 111 us
  Pallas kernels  105 us (95%)
  local copies, waits for them, and re-layouts  5.84 us (5%)
    pallas_call x1, Pallas kernels, body(): pl.pallas_call(functools.partial(kernel, n, A, B, wx, cuts, tile), out_sh...  105 us
    unnamed x1, local copies, waits for them, and re-layouts  3.13 us

profile of v2, /device:TPU:0, one launch (start us, length us, event | category | flops | bytes accessed | tf_op | source)
XLA Modules:
  0.0 110.6 jit_solution(15347996020528672045)
XLA Ops:
  0.0 1.3 %broadcast_in_dim.4.seg_row_ref = s32[8,256]{1,0:T(8,128)} broadcast(s32[256]{0:T(256)} %param.8), dimensions={1} | broadcast | bytes 9216 | tf_op jit(solution)/shard_map/broadcast_in_dim | solution.py:298
  1.3 1.4 %broadcast_in_dim.5.seg_col_ref = s32[256,128]{1,0:T(8,128)} broadcast(s32[256]{0:T(256)} %param.8), dimensions={0} | broadcast | bytes 132096 | tf_op jit(solution)/shard_map/broadcast_in_dim | solution.py:299
  2.7 104.8 %shard_map.55 = bf16[256,4096]{1,0:T(8,128)(2,1)} custom-call(bf16[256,2048]{1,0:T(8,128)(2,1)} %q_ref.1, bf16[256,512]{1,0:T(8,128)(2,1)} %k_ref.1, bf16[256,512]{1,0:T(8,128)(2,1)} %v_ref.1, s32[8,256]{1,0:T(8,128)} %broadcast_in_dim.4.seg_row_ref, s32[256,128]{1,0:T(8,128)} %broadcast_in_dim.5.seg_col_ref, bf16[128,4096]{1,0:T(8,128)(2,1)} %w_ref.1), custom_call_target="tpu_custom_call" | custom-call | flops 6442450944 | bytes 4194304 | tf_op jit(solution)/shard_map/pallas_call | solution.py:302
  107.5 3.1 %copy.7 = bf16[256,4096]{1,0:T(8,128)(2,1)} copy(bf16[256,4096]{1,0:T(8,128)(2,1)} %shard_map.55) | data formatting | bytes 4194304

commit v3 on v2

--- a/solution.py
+++ b/solution.py
@@ -22,7 +22,7 @@
     return chips // b, b
 
 
-def kernel(n, A, B, wx, cuts, tile,
+def kernel(n, A, B, wx, tile,
            q_ref, k_ref, v_ref, seg_row_ref, seg_col_ref, w_ref, out_ref,
            W, kwin, vwin, swin, bias, att,
            send, recv, kv_send, kv_recv):
@@ -39,16 +39,11 @@
     def index(a_, b_, c_):
         return (a_ * B + b_) * CORES + c_
 
-    part = wx // cuts
-    rest = width - 2 * wx
-    MINE = tuple(range(cuts))
-    BOTH = (cuts,)
-    THEIRS = tuple(range(cuts + 1, 2 * cuts + 1))
-    widths = (part,) * cuts + (rest,) + (part,) * cuts
-    starts = (tuple(g * wx + j * part for j in range(cuts)) + (2 * wx,)
-              + tuple((1 - g) * wx + j * part for j in range(cuts)))
-    number = (tuple(g * cuts + j for j in range(cuts)) + (2 * cuts,)
-              + tuple((1 - g) * cuts + j for j in range(cuts)))
+    half = (width - 2 * wx) // (2 * tile) * tile
+    MINE, BOTH, TURNED, THEIRS = (0,), (1,), (2,), (3,)
+    widths = (wx, width - 2 * wx - half, half, wx)
+    starts = (g * wx, 2 * wx, width - half, (1 - g) * wx)
+    number = (g, 2, 3, 1 - g)
 
     def move(p, s, way, device):
         view = W.at[pl.ds(pl.multiple_of(s * depth, depth), depth),
@@ -121,6 +116,31 @@
         else:
             pl.when(a - t >= 0)(lambda: column(a - t))
             pl.when(a + t < A)(lambda: column(a + t))
+
+    def turned(p, t, mode):
+        def take(a_, b_, ways):
+            s = index(a_, b_, c)
+            arrive(p, s, mode)
+            for way, device, more in ways:
+                pl.when(more)(functools.partial(
+                    lambda way, device: act(move(p, s, way, device), mode), way, device))
+            act(move(p, s, SIBLING, sibling), mode)
+
+        up = (UP_A, up_a, a + 1 < A)
+        down = (DOWN_A, down_a, a > 0)
+
+        def step(u, carry):
+            if t == 0:
+                pl.when(b - u >= 0)(lambda: take(
+                    a, b - u, ((UP_B, up_b, b + 1 < B), up, down)))
+                pl.when(b + u < B)(lambda: take(
+                    a, b + u, ((DOWN_B, down_b, b > 0), up, down)))
+            else:
+                pl.when(a - t >= 0)(lambda: take(a - t, u, (up,)))
+                pl.when(a + t < A)(lambda: take(a + t, u, (down,)))
+            return carry
+
+        lax.fori_loop(1 if t == 0 else 0, B, step, 0)
 
     def from_across(p, t, mode):
         def column(a_):
@@ -184,7 +204,7 @@
     for way in (0, 2):
         for copy in kv_copies(way):
             copy.start()
-    own(BOTH, "start")
+    own(BOTH + TURNED, "start")
     for p in THEIRS:
         move(p, i, SIBLING, sibling).start()
 
@@ -225,10 +245,14 @@
 
     done = 0
     for t in range(A):
-        for p in MINE + BOTH:
-            if t > 0:
+        if t > 0:
+            for p in MINE + BOTH:
                 from_a(p, t, "start")
-            from_b(p, t, "start")
+        for p in MINE + TURNED + BOTH:
+            if p in TURNED:
+                turned(p, t, "start")
+            else:
+                from_b(p, t, "start")
         if t == 0:
             for copy in slot(1):
                 copy.wait_recv()
@@ -268,10 +292,10 @@
         project(p)
     for p in THEIRS:
         from_across(p, A - 1, "start")
-    for p in BOTH + THEIRS:
+    for p in BOTH + TURNED + THEIRS:
         project(p)
 
-    own(MINE + BOTH, "wait")
+    own(MINE + BOTH + TURNED, "wait")
     for p in THEIRS:
         move(p, i, SIBLING, sibling).wait_send()
     for t in range(A):
@@ -279,6 +303,8 @@
             if t > 0:
                 from_a(p, t, "wait")
             from_b(p, t, "wait")
+        for p in TURNED:
+            turned(p, t, "wait")
         for p in THEIRS:
             from_across(p, t, "wait")
     for way in range(3):
@@ -293,14 +319,13 @@
     width = out_weight.shape[1]
     A, B = grid_of(n)
     tile = math.gcd(width, 512)
-    cuts = 1
-    wx = width * 3 // 8 // (cuts * tile) * (cuts * tile)
+    wx = width * 3 // 8 // tile * tile
     seg_row = jnp.broadcast_to(segment[None, :], (8, rows))
     seg_col = jnp.broadcast_to(segment[:, None], (rows, 128))
     vmem = pl.BlockSpec(memory_space=pltpu.VMEM)
     window = rows * SPAN
     return pl.pallas_call(
-        functools.partial(kernel, n, A, B, wx, cuts, tile),
+        functools.partial(kernel, n, A, B, wx, tile),
         out_shape=jax.ShapeDtypeStruct((rows, width), jnp.bfloat16),
         in_specs=[vmem] * 6,
         out_specs=vmem,
@@ -311,8 +336,8 @@
             pltpu.VMEM((SPAN, 8, rows), jnp.int32),
             pltpu.VMEM((rows, window), jnp.float32),
             pltpu.VMEM((rows, q_width), jnp.bfloat16),
-            pltpu.SemaphoreType.DMA((6, 2 * cuts + 1, n)),
-            pltpu.SemaphoreType.DMA((2 * cuts + 1, n)),
+            pltpu.SemaphoreType.DMA((6, 4, n)),
+            pltpu.SemaphoreType.DMA((4, n)),
             pltpu.SemaphoreType.DMA((SPAN - 1, 3)),
             pltpu.SemaphoreType.DMA((SPAN - 1, 3)),
         ],

time: 111 us -> 106 us (0.955)
  the two profiles are of different devices: /device:TPU:0 before, /device:TPU:16 now
where the time goes in v3:
time: 106 us
  Pallas kernels  100 us (94%)
  local copies, waits for them, and re-layouts  5.84 us (6%)
    pallas_call x1, Pallas kernels, body(): pl.pallas_call(functools.partial(kernel, n, A, B, wx, tile), out_shape=ja...  100 us
    unnamed x1, local copies, waits for them, and re-layouts  3.13 us

profile of v3, /device:TPU:16, one launch (start us, length us, event | category | flops | bytes accessed | tf_op | source)
XLA Modules:
  0.0 106.2 jit_solution(1858850362779727048)
XLA Ops:
  0.0 1.3 %broadcast_in_dim.4.seg_row_ref = s32[8,256]{1,0:T(8,128)} broadcast(s32[256]{0:T(256)} %param.8), dimensions={1} | broadcast | bytes 9216 | tf_op jit(solution)/shard_map/broadcast_in_dim | solution.py:323
  1.3 1.4 %broadcast_in_dim.5.seg_col_ref = s32[256,128]{1,0:T(8,128)} broadcast(s32[256]{0:T(256)} %param.8), dimensions={0} | broadcast | bytes 132096 | tf_op jit(solution)/shard_map/broadcast_in_dim | solution.py:324
  2.7 100.3 %shard_map.55 = bf16[256,4096]{1,0:T(8,128)(2,1)} custom-call(bf16[256,2048]{1,0:T(8,128)(2,1)} %q_ref.1, bf16[256,512]{1,0:T(8,128)(2,1)} %k_ref.1, bf16[256,512]{1,0:T(8,128)(2,1)} %v_ref.1, s32[8,256]{1,0:T(8,128)} %broadcast_in_dim.4.seg_row_ref, s32[256,128]{1,0:T(8,128)} %broadcast_in_dim.5.seg_col_ref, bf16[128,4096]{1,0:T(8,128)(2,1)} %w_ref.1), custom_call_target="tpu_custom_call" | custom-call | flops 6442450944 | bytes 4194304 | tf_op jit(solution)/shard_map/pallas_call | solution.py:327
  103.0 3.1 %copy.7 = bf16[256,4096]{1,0:T(8,128)(2,1)} copy(bf16[256,4096]{1,0:T(8,128)(2,1)} %shard_map.55) | data formatting | bytes 4194304

commit v4 on v3

--- a/solution.py
+++ b/solution.py
@@ -248,7 +248,7 @@
         if t > 0:
             for p in MINE + BOTH:
                 from_a(p, t, "start")
-        for p in MINE + TURNED + BOTH:
+        for p in MINE + TURNED + BOTH if t == 0 else TURNED + MINE + BOTH:
             if p in TURNED:
                 turned(p, t, "start")
             else:
@@ -264,11 +264,11 @@
                     copy.wait_recv()
             mask()
         if t > 0:
-            for p in THEIRS:
-                from_across(p, t - 1, "start")
             if done < KV_HEADS:
                 attend(done)
                 done += 1
+            for p in THEIRS:
+                from_across(p, t - 1, "start")
     for kv in range(done, KV_HEADS):
         attend(kv)
 

time: 106 us -> 104 us (0.981)
  the two profiles are of different devices: /device:TPU:16 before, /device:TPU:0 now
where the time goes in v4:
time: 104 us
  Pallas kernels  97.9 us (94%)
  local copies, waits for them, and re-layouts  5.84 us (6%)
    pallas_call x1, Pallas kernels, body(): pl.pallas_call(functools.partial(kernel, n, A, B, wx, tile), out_shape=ja...  97.9 us
    unnamed x1, local copies, waits for them, and re-layouts  3.13 us

profile of v4, /device:TPU:0, one launch (start us, length us, event | category | flops | bytes accessed | tf_op | source)
XLA Modules:
  0.0 103.7 jit_solution(14428106639688653347)
XLA Ops:
  0.0 1.3 %broadcast_in_dim.4.seg_row_ref = s32[8,256]{1,0:T(8,128)} broadcast(s32[256]{0:T(256)} %param.8), dimensions={1} | broadcast | bytes 9216 | tf_op jit(solution)/shard_map/broadcast_in_dim | solution.py:323
  1.3 1.4 %broadcast_in_dim.5.seg_col_ref = s32[256,128]{1,0:T(8,128)} broadcast(s32[256]{0:T(256)} %param.8), dimensions={0} | broadcast | bytes 132096 | tf_op jit(solution)/shard_map/broadcast_in_dim | solution.py:324
  2.7 97.9 %shard_map.55 = bf16[256,4096]{1,0:T(8,128)(2,1)} custom-call(bf16[256,2048]{1,0:T(8,128)(2,1)} %q_ref.1, bf16[256,512]{1,0:T(8,128)(2,1)} %k_ref.1, bf16[256,512]{1,0:T(8,128)(2,1)} %v_ref.1, s32[8,256]{1,0:T(8,128)} %broadcast_in_dim.4.seg_row_ref, s32[256,128]{1,0:T(8,128)} %broadcast_in_dim.5.seg_col_ref, bf16[128,4096]{1,0:T(8,128)(2,1)} %w_ref.1), custom_call_target="tpu_custom_call" | custom-call | flops 6442450944 | bytes 4194304 | tf_op jit(solution)/shard_map/pallas_call | solution.py:327
  100.6 3.1 %copy.7 = bf16[256,4096]{1,0:T(8,128)(2,1)} copy(bf16[256,4096]{1,0:T(8,128)(2,1)} %shard_map.55) | data formatting | bytes 4194304
